TPU v7x, 256 devices: a whole 4x4x8 slice. The times are simulated.
256 devices in a mesh: row: 8 (over z_lo, core), col: 32 (over y, z_hi, x).
Axes of the slice: x: 4, y: 4, z: 8 (z_hi: 2, z_lo: 4; z = z_hi * 4 + z_lo), core: 2. Of those that a mesh axis runs over, the one named last changes fastest.
Arguments:
- spectra: bfloat16 [4, 1024, 8192], P(None, 'col', 'row'), may hold values from -6 to 6
- valid: int32 [1024, 8192], P('col', 'row'), may hold values 0 or 1
Outputs:
- cross: float32 [2, 2, 8192, 8192], P(None, None, 'row', 'col')
All inputs are finite; a program needn't handle non-finite values. No bound on the sum of `valid` on one device may be relied on, other than what follows from the above.
Results may differ from a plain program's by a relative error of at most 0.003.
Values may be sent and summed in bfloat16 or wider, within the bound.
A program may use at most 128 MiB of HBM per device.

v0:
```python
import jax
import jax.numpy as jnp
from jax import lax
from jax.sharding import PartitionSpec as P


def spread(value, axis, source):
    kept = jnp.where(lax.axis_index(axis) == source, value, 0).astype(value.dtype)
    return lax.psum(kept, axis)


def whiten(spectra, valid):
    values = spectra.astype(jnp.float32)
    real_part = values[0::2]
    imag_part = values[1::2]
    amplitude = jnp.sqrt(real_part * real_part + imag_part * imag_part)
    factor = valid.astype(jnp.float32)[None] / jnp.maximum(amplitude, 0.5)
    stacked = jnp.stack([real_part * factor, imag_part * factor], axis=1)
    return stacked.reshape(values.shape).astype(jnp.bfloat16)


def pair_dot(left, right):
    return lax.dot_general(
        left, right, (((0,), (0,)), ((), ())), preferred_element_type=jnp.float32
    )


def on_device(spectra, valid):
    white = whiten(spectra, valid)
    gathered = lax.all_gather(white, "col", axis=1, tiled=True)
    ratio = lax.axis_size("col") // lax.axis_size("row")
    block_rows = gathered.shape[2]
    width = block_rows // ratio
    column = lax.axis_index("col")
    owner = column // ratio
    offset = column % ratio * width
    received = spread(gathered, "row", owner)
    partner = lax.dynamic_slice_in_dim(received, offset, width, 2)
    windows = gathered.shape[1]
    norm = 1.0 / jnp.sqrt(jnp.float32(windows))
    real_out = []
    imag_out = []
    for freq in range(gathered.shape[0] // 2):
        real_rows = gathered[2 * freq]
        imag_rows = gathered[2 * freq + 1]
        real_cols = partner[2 * freq]
        imag_cols = partner[2 * freq + 1]
        real_out.append((pair_dot(real_rows, real_cols) + pair_dot(imag_rows, imag_cols)) * norm)
        imag_out.append((pair_dot(imag_rows, real_cols) - pair_dot(real_rows, imag_cols)) * norm)
    return jnp.stack([jnp.stack(real_out), jnp.stack(imag_out)])


def solution(mesh):
    placed = (P(None, "col", "row"), P("col", "row"))
    return jax.shard_map(
        on_device,
        mesh=mesh,
        in_specs=placed,
        out_specs=P(None, None, "row", "col"),
        check_vma=False,
    )
```

profile of v0, /device:TPU:48, one launch (start us, length us, event | category | flops | bytes accessed | tf_op | source)
XLA Modules:
  0.0 382.1 jit_solution(3582361134976365029)
XLA Ops:
  6.5 0.0 all-gather.2.cloned.1.call-start
  6.5 1.0 convert_element_type.12
  7.5 0.9 convert_element_type.13
  8.5 0.1 fusion.20
  8.6 0.7 pad_maximum_fusion.1
  9.3 0.0 all-gather.2.cloned.1.call-update
  9.4 0.0 all-reduce.2.cloned.1.call-start
  9.4 158.2 %all-gather.2.cloned.1.call-done = bf16[4,1024,1024]{2,1,0:T(8,128)(2,1)} async-done(((bf16[4,32,1024]{2,1,0:T(8,128)(2,1)}), bf16[4,1024,1024]{2,1,0:T(8,128)(2,1)}) %all-gather.2.cloned.1.call-update) | async-done | bytes 8388624 | tf_op jit(solution)/shard_map/all_gather | solution.py:30
  167.7 3.8 broadcast_select_fusion
  171.4 0.0 all-reduce.2.cloned.1.call-update
  171.5 184.0 %all-reduce.2.cloned.1.call-done = bf16[4,1024,1024]{2,1,0:T(8,128)(2,1)} async-done(((bf16[4,1024,1024]{2,1,0:T(8,128)(2,1)}), bf16[4,1024,1024]{2,1,0:T(8,128)(2,1)}) %all-reduce.2.cloned.1.call-update) | async-done | bytes 8388624 | tf_op jit(solution)/shard_map/psum | solution.py:9
  355.4 2.4 fusion.1
  357.9 0.0 slice-start
  357.9 2.6 fusion
  360.4 0.0 slice-start.1
  360.5 2.6 fusion.19
  363.1 0.5 slice-done.1
  363.5 1.8 fusion.4
  365.3 1.8 fusion.5
  367.1 1.8 fusion.13
  368.9 1.8 fusion.16
  370.8 1.8 fusion.10
  372.6 0.4 maximum_bitcast_fusion
  372.9 2.3 pad_maximum_fusion
  (2 shorter events, 0.0 us)
Async XLA Ops:
  6.5 161.1 %all-gather.2.cloned.1.call-start = ((), (), s32[]{:S(2)}) async-start(), calls=%async_computation | async-start | bytes 8650752 | tf_op jit(solution)/shard_map/all_gather | solution.py:30
  9.4 346.1 %all-reduce.2.cloned.1.call-start = ((), (), s32[]{:S(2)}) async-start(), calls=%async_computation.1 | async-start | bytes 16777216 | tf_op jit(solution)/shard_map/psum | solution.py:9
  357.9 5.2 %slice-start = ((s8[8388608]{0:T(1024)(128)(4,1)}), s8[4194304]{0:T(1024)(128)(4,1)S(1)}, s32[]{:S(2)}) async-start(s8[8388608]{0:T(1024)(128)(4,1)} %bitcast.75), calls=%async_computation.2 | async-start | bytes 8388608
  360.4 3.1 slice-start.1
Sparse Core Ops, SparseCore 0:
  10.9 156.6 all-gather.1
  171.6 183.8 all-reduce.1
where the time goes:
time: 386 us; the launch traced here: 382 us
  waiting for transfers between devices  342 us (89%)
  matrix products  16.6 us (4%)
  between operations  13.5 us (3%)
  other arithmetic  9.2 us (2%)
    psum x1, waiting for transfers between devices, spread(): return lax.psum(kept, axis)  184 us
    all_gather x1, waiting for transfers between devices, on_device(): gathered = lax.all_gather(white, 'col', axis=1, tiled=True)  158 us
    dot_general x8, matrix products, pair_dot(): lax.dot_general(left, right, (((0,), (0,)), ((), ())), preferred_element_...  16.6 us
  transfers between devices with their start and end apart: 2, of which 2 were waited for; matrix products, arithmetic and copies ran while one was open for 0% of the time, Pallas kernels for 0%

commit v1 on v0

v1 whole, which is shorter than its diff:
```python
import functools

import jax
import jax.numpy as jnp
from jax import lax
from jax.experimental import pallas as pl
from jax.experimental.pallas import tpu as pltpu
from jax.sharding import PartitionSpec as P

MESH = pl.DeviceIdType.MESH
RING = 4
LINE = 8


def device(x, y, z, core):
    return (lax.rem(z, 4) * 2 + core, y * 8 + lax.div(z, 4) * 4 + x)


def up(a, d, n):
    return lax.rem(a + (d + n), n)


def kernel(norm, spectra, valid, out, gathered, partner, z_send, z_recv, in_send, in_recv,
           out_send, out_recv, b_send, b_pass, b_side, b_recv):
    row = lax.axis_index("row")
    col = lax.axis_index("col")
    core = lax.rem(row, 2)
    low = lax.div(row, 2)
    x = lax.rem(col, 4)
    half = lax.rem(lax.div(col, 4), 2)
    y = lax.div(col, 8)
    z = half * 4 + low
    width = partner.shape[-1]
    windows = spectra.shape[1]
    lanes = pl.ds(pl.multiple_of(x * width, width), width)
    place = ((x, y), (y, x))

    def ring_device(f, inner, step):
        if (f == 0) == inner:
            return device(up(x, step, RING), y, z, core)
        return device(x, up(y, step, RING), z, core)

    sibling = device(x, y, z, 1 - core)

    barrier = pltpu.get_barrier_semaphore()
    greeted = [ring_device(0, inner, step) for inner in (True, False) for step in (1, -1)]
    greeted += [device(x, y, up(z, d, LINE), c) for d in range(1, LINE) for c in range(2)]
    greeted.append(sibling)
    for other in greeted:
        pl.semaphore_signal(barrier, inc=1, device_id=other, device_id_type=MESH)

    for f in range(2):
        real = spectra[2 * f].astype(jnp.float32)
        imag = spectra[2 * f + 1].astype(jnp.float32)
        amplitude = jnp.sqrt(real * real + imag * imag)
        factor = valid[...].astype(jnp.float32) / jnp.maximum(amplitude, 0.5)
        inner, outer = place[f]
        gathered[f, half, outer, inner, 0] = (real * factor).astype(jnp.bfloat16)
        gathered[f, half, outer, inner, 1] = (imag * factor).astype(jnp.bfloat16)
    pl.semaphore_wait(barrier, len(greeted))

    pending = []

    def send(ref, send_sem, recv_sem, target, landing=None, when=None):
        copy = pltpu.make_async_remote_copy(
            src_ref=ref,
            dst_ref=ref if landing is None else landing,
            send_sem=send_sem,
            recv_sem=recv_sem,
            device_id=target,
            device_id_type=MESH,
        )
        if when is None:
            copy.start()
        else:
            pl.when(when)(copy.start)
        pending.append((copy, when))

    def arrived(ref, recv_sem):
        pltpu.make_async_remote_copy(
            src_ref=ref,
            dst_ref=ref,
            send_sem=z_send.at[0],
            recv_sem=recv_sem,
            device_id=sibling,
            device_id_type=MESH,
        ).wait_recv()

    def side(r):
        return half if r == 0 else 1 - half

    inner_steps = (0, -1, 1, 2)

    def slot(f, r, do, di):
        inner, outer = place[f]
        return gathered.at[f, side(r), up(outer, do, RING), up(inner, di, RING)]

    def outer_send(f, r, j):
        block = slot(f, r, 0, inner_steps[j])
        for k, step in enumerate((1, -1)):
            send(block, out_send.at[r, f, k, j], out_recv.at[r, f, k, j], ring_device(f, False, step))

    def inner_start(f, r):
        block = slot(f, r, 0, 0)
        for k, step in enumerate((1, -1)):
            send(block, in_send.at[r, f, k], in_recv.at[r, f, k], ring_device(f, True, step))

    def inner_forward(f, r):
        for k, step in enumerate((1, -1)):
            block = slot(f, r, 0, -step)
            arrived(block, in_recv.at[r, f, k])
            send(block.at[k], in_send.at[r, f, 2 + k], in_recv.at[r, f, 2 + k], ring_device(f, True, step))
            outer_send(f, r, 1 + k)

    def inner_finish(f, r):
        block = slot(f, r, 0, 2)
        for k in range(2):
            arrived(block.at[k], in_recv.at[r, f, 2 + k])
        outer_send(f, r, 3)

    def outer_forward(f, r, j):
        for k, step in enumerate((1, -1)):
            block = slot(f, r, -step, inner_steps[j])
            arrived(block, out_recv.at[r, f, k, j])
            send(block.at[k], out_send.at[r, f, 2 + k, j], out_recv.at[r, f, 2 + k, j], ring_device(f, False, step))

    def outer_finish(f, r):
        for j in range(4):
            block = slot(f, r, 2, inner_steps[j])
            for k in range(2):
                arrived(block.at[k], out_recv.at[r, f, 2 + k, j])

    diagonal = low == y
    owner = jnp.logical_and(diagonal, core == half)
    outer_steps = (0, -1, 1, 2)

    def half_of(d):
        return lax.div(up(z, d, LINE), 4)

    def b_slot(f, h, rel):
        return partner.at[f, h, up(place[f][1], outer_steps[rel], RING)]

    def b_source(f, r, rel):
        return gathered.at[f, side(r), up(place[f][1], outer_steps[rel], RING), :, :, :, lanes]

    def b_start(f, rel):
        for k, step in enumerate((1, -1)):
            first = half_of(step) == core
            second = half_of(2 * step) == core
            third = half_of(3 * step) == core
            distance = jnp.where(first, 1, jnp.where(second, 2, 3))
            found = jnp.logical_or(first, jnp.logical_or(second, third))
            target = device(x, y, lax.rem(z + distance * step + LINE, LINE), f)
            send(b_source(f, 0, rel), b_send.at[k, f, rel], b_recv.at[half_index(0), f, rel], target,
                 landing=b_slot(f, half, rel), when=jnp.logical_and(diagonal, found))

    def half_index(r):
        return side(r)

    def b_local(f, r, rel):
        copy = pltpu.make_async_copy(b_source(f, r, rel), b_slot(f, side(r), rel), b_recv.at[side(r), f, rel])
        pl.when(owner)(copy.start)
        send(b_source(f, r, rel), b_side.at[r, f, rel], b_recv.at[side(r), f, rel], sibling,
             landing=b_slot(f, side(r), rel), when=owner)

    def b_wait(f, r, rel):
        block = b_slot(f, side(r), rel)
        arrived(block, b_recv.at[side(r), f, rel])

    def b_relay(f, r, rel):
        h = side(r)
        block = b_slot(f, h, rel)

        @pl.when(jnp.logical_not(diagonal))
        def _():
            b_wait(f, r, rel)

        mine = jnp.logical_and(jnp.logical_not(diagonal), core == f)
        send(block, b_side.at[r, f, rel], b_recv.at[h, f, rel], sibling, when=mine)
        distance = lax.rem(z - (y + 4 * h) + 2 * LINE, LINE)
        step = jnp.where(distance < 4, 1, -1)
        following = lax.rem(z + step + LINE, LINE)
        goes_on = jnp.logical_and(
            jnp.logical_and(distance != 3, distance != 5), lax.div(following, 4) == half
        )
        send(block, b_pass.at[r, f, rel], b_recv.at[h, f, rel], device(x, y, following, core),
             when=jnp.logical_and(mine, goes_on))

    def chunk(f, r, rel, first=False, last=False):
        h = side(r)
        outer = up(place[f][1], outer_steps[rel], RING)
        depth = RING * 2 * windows
        block = partner[f, h, outer]
        turned = jnp.stack([-block[:, 1], block[:, 0]], axis=1)
        right = jnp.concatenate([block.reshape(depth, width), turned.reshape(depth, width)], axis=1)
        tile = 256

        @pl.loop(0, gathered.shape[-1] // tile)
        def _(t):
            rows = pl.ds(pl.multiple_of(t * tile, tile), tile)
            left = gathered[f, h, outer, :, :, :, rows].reshape(depth, tile)
            product = lax.dot_general(
                left, right, (((0,), (0,)), ((), ())), preferred_element_type=jnp.float32
            )
            for p in range(2):
                part = product[:, p * width:(p + 1) * width]
                if not first:
                    part = out[p, f, rows, :] + part
                if last:
                    part = part * norm
                out[p, f, rows, :] = part

    both = range(2)
    for f in both:
        send(slot(f, 0, 0, 0), z_send.at[f], z_recv.at[f], device(x, y, up(z, 4, LINE), core))
        inner_start(f, 0)
    for f in both:
        outer_send(f, 0, 0)
    for f in both:
        inner_forward(f, 0)
    for f in both:
        inner_finish(f, 0)
        b_start(f, 0)
        b_local(f, 0, 0)
    for f in both:
        outer_forward(f, 0, 0)
    for f in both:
        outer_forward(f, 0, 1)
    for f in both:
        arrived(slot(f, 1, 0, 0), z_recv.at[f])
        inner_start(f, 1)
        outer_send(f, 1, 0)
    for f in both:
        outer_forward(f, 0, 2)
    for f in both:
        for r in range(2):
            b_relay(f, r, 0)
    for f in both:
        outer_forward(f, 0, 3)
        for rel in (1, 2):
            b_start(f, rel)
            b_local(f, 0, rel)
    for f in both:
        inner_forward(f, 1)
    for f in both:
        outer_finish(f, 0)
        b_start(f, 3)
        b_local(f, 0, 3)
    for f in both:
        inner_finish(f, 1)
        b_local(f, 1, 0)

    def own_wait(f, r, rel):
        pl.when(diagonal)(functools.partial(b_wait, f, r, rel))

    for f in both:
        outer_forward(f, 1, 0)
        own_wait(f, 0, 0)
        chunk(f, 0, 0, first=True)
    for rel in (1, 2):
        for f in both:
            for r in range(2):
                b_relay(f, r, rel)
            outer_forward(f, 1, rel)
            own_wait(f, 0, rel)
            chunk(f, 0, rel)
    for f in both:
        for r in range(2):
            b_relay(f, r, 3)
        outer_forward(f, 1, 3)
    for f in both:
        for rel in (1, 2):
            b_local(f, 1, rel)
        own_wait(f, 0, 3)
        chunk(f, 0, 3)
    for rel in (0, 1, 2):
        for f in both:
            own_wait(f, 1, rel)
            chunk(f, 1, rel)
    for f in both:
        outer_finish(f, 1)
        b_local(f, 1, 3)
        own_wait(f, 1, 3)
        chunk(f, 1, 3, last=True)

    for copy, when in pending:
        if when is None:
            copy.wait_send()
        else:
            pl.when(when)(copy.wait_send)


def on_device(spectra, valid):
    planes, windows, rows = spectra.shape
    width = rows // 4
    total = windows * lax.axis_size("col")
    norm = 1.0 / float(total) ** 0.5
    dma = pltpu.SemaphoreType.DMA
    vmem = pl.BlockSpec(memory_space=pltpu.VMEM)
    return pl.pallas_call(
        functools.partial(kernel, norm),
        out_shape=jax.ShapeDtypeStruct((2, planes // 2, rows, width), jnp.float32),
        in_specs=[vmem, vmem],
        out_specs=vmem,
        scratch_shapes=[
            pltpu.VMEM((2, 2, RING, RING, 2, windows, rows), jnp.bfloat16),
            pltpu.VMEM((2, 2, RING, RING, 2, windows, width), jnp.bfloat16),
            dma((2,)),
            dma((2,)),
            dma((2, 2, 4)),
            dma((2, 2, 4)),
            dma((2, 2, 4, 4)),
            dma((2, 2, 4, 4)),
            dma((2, 2, 4)),
            dma((2, 2, 4)),
            dma((2, 2, 4)),
            dma((2, 2, 4)),
        ],
        compiler_params=pltpu.CompilerParams(
            collective_id=0, has_side_effects=True, vmem_limit_bytes=48 * 2**20
        ),
        cost_estimate=pl.CostEstimate(
            flops=16 * total * rows * width, bytes_accessed=2**22, transcendentals=0
        ),
    )(spectra, valid)


def solution(mesh):
    placed = (P(None, "col", "row"), P("col", "row"))
    return jax.shard_map(
        on_device,
        mesh=mesh,
        in_specs=placed,
        out_specs=P(None, None, "row", "col"),
        check_vma=False,
    )
```

time: 386 us -> 178 us (0.46)
  the two profiles are of different devices: /device:TPU:48 before, /device:TPU:32 now
where the time goes in v1:
time: 178 us
  Pallas kernels  174 us (98%)
  local copies, waits for them, and re-layouts  3.87 us (2%)
    pallas_call x1, Pallas kernels, on_device(): pl.pallas_call(functools.partial(kernel, norm), out_shape=jax.ShapeDtypeS...  174 us
    unnamed x5, local copies, waits for them, and re-layouts  3.87 us

profile of v1, /device:TPU:32, one launch (start us, length us, event | category | flops | bytes accessed | tf_op | source)
XLA Modules:
  0.0 177.5 jit_solution(7029454771791392754)
XLA Ops:
  0.0 0.0 copy-start
  0.0 0.9 copy-done
  1.0 0.0 copy-start.1
  1.0 0.9 copy-done.1
  1.9 173.6 %shard_map.28 = f32[2,2,1024,256]{3,2,1,0:T(8,128)S(1)} custom-call(bf16[4,32,1024]{2,1,0:T(8,128)(2,1)S(1)} %copy-done, s32[32,1024]{1,0:T(8,128)S(1)} %copy-done.1), custom_call_target="tpu_custom_call" | custom-call | flops 4294967296 | bytes 4194304 | tf_op jit(solution)/shard_map/pallas_call | solution.py:300
  175.5 2.0 %copy.4 = f32[2,2,1024,256]{3,2,1,0:T(8,128)} copy(f32[2,2,1024,256]{3,2,1,0:T(8,128)S(1)} %shard_map.28) | data formatting | bytes 8388608
Async XLA Ops:
  0.0 0.9 copy-start
  1.0 0.9 copy-start.1

commit v2 on v1

--- a/solution.py
+++ b/solution.py
@@ -21,7 +21,7 @@
 
 
 def kernel(norm, spectra, valid, out, gathered, partner, z_send, z_recv, in_send, in_recv,
-           out_send, out_recv, b_send, b_pass, b_side, b_recv):
+           out_send, out_recv, b_send, b_pass, b_far, b_side, b_recv):
     row = lax.axis_index("row")
     col = lax.axis_index("col")
     core = lax.rem(row, 2)
@@ -145,17 +145,14 @@
 
     def b_start(f, rel):
         for k, step in enumerate((1, -1)):
-            first = half_of(step) == core
-            second = half_of(2 * step) == core
-            third = half_of(3 * step) == core
-            distance = jnp.where(first, 1, jnp.where(second, 2, 3))
-            found = jnp.logical_or(first, jnp.logical_or(second, third))
-            target = device(x, y, lax.rem(z + distance * step + LINE, LINE), f)
-            send(b_source(f, 0, rel), b_send.at[k, f, rel], b_recv.at[half_index(0), f, rel], target,
-                 landing=b_slot(f, half, rel), when=jnp.logical_and(diagonal, found))
-
-    def half_index(r):
-        return side(r)
+            fits = [half_of(d * step) == core for d in (1, 2, 3)]
+            nearest = jnp.where(fits[0], 1, jnp.where(fits[1], 2, 3))
+            found = jnp.logical_or(fits[0], jnp.logical_or(fits[1], fits[2]))
+            third = jnp.logical_and(fits[0], fits[2])
+            for n, (distance, when) in enumerate(((nearest, found), (3, third))):
+                target = device(x, y, lax.rem(z + distance * step + LINE, LINE), f)
+                send(b_source(f, 0, rel), b_send.at[k, n, f, rel], b_recv.at[half, f, rel], target,
+                     landing=b_slot(f, half, rel), when=jnp.logical_and(diagonal, when))
 
     def b_local(f, r, rel):
         copy = pltpu.make_async_copy(b_source(f, r, rel), b_slot(f, side(r), rel), b_recv.at[side(r), f, rel])
@@ -164,27 +161,32 @@
              landing=b_slot(f, side(r), rel), when=owner)
 
     def b_wait(f, r, rel):
-        block = b_slot(f, side(r), rel)
-        arrived(block, b_recv.at[side(r), f, rel])
-
-    def b_relay(f, r, rel):
+        arrived(b_slot(f, side(r), rel), b_recv.at[side(r), f, rel])
+
+    def b_place(r):
+        distance = lax.rem(z - (y + 4 * side(r)) + 2 * LINE, LINE)
+        step = jnp.where(distance < 4, 1, -1)
+        steps = jnp.where(distance < 4, distance, LINE - distance)
+        before = lax.rem(z - step + LINE, LINE)
+        after = lax.rem(z + step + LINE, LINE)
+        nearest = jnp.logical_or(steps == 1, lax.div(before, 4) != half)
+        goes_on = jnp.logical_and(nearest, jnp.logical_and(steps != 3, lax.div(after, 4) == half))
+        return nearest, goes_on, after
+
+    def b_pass_on(f, r, rel, nearest):
         h = side(r)
         block = b_slot(f, h, rel)
-
-        @pl.when(jnp.logical_not(diagonal))
-        def _():
-            b_wait(f, r, rel)
-
+        is_nearest, goes_on, after = b_place(r)
         mine = jnp.logical_and(jnp.logical_not(diagonal), core == f)
-        send(block, b_side.at[r, f, rel], b_recv.at[h, f, rel], sibling, when=mine)
-        distance = lax.rem(z - (y + 4 * h) + 2 * LINE, LINE)
-        step = jnp.where(distance < 4, 1, -1)
-        following = lax.rem(z + step + LINE, LINE)
-        goes_on = jnp.logical_and(
-            jnp.logical_and(distance != 3, distance != 5), lax.div(following, 4) == half
-        )
-        send(block, b_pass.at[r, f, rel], b_recv.at[h, f, rel], device(x, y, following, core),
-             when=jnp.logical_and(mine, goes_on))
+        mine = jnp.logical_and(mine, is_nearest if nearest else jnp.logical_not(is_nearest))
+        pl.when(mine)(functools.partial(b_wait, f, r, rel))
+        if nearest:
+            send(block, b_pass.at[r, f, rel], b_recv.at[h, f, rel], device(x, y, after, core),
+                 when=jnp.logical_and(mine, goes_on))
+        send(block, b_far.at[int(nearest), r, f, rel], b_recv.at[h, f, rel], sibling, when=mine)
+
+    def b_need(f, r, rel):
+        pl.when(jnp.logical_or(diagonal, core != f))(functools.partial(b_wait, f, r, rel))
 
     def chunk(f, r, rel, first=False, last=False):
         h = side(r)
@@ -211,6 +213,28 @@
                 out[p, f, rows, :] = part
 
     both = range(2)
+
+    def b_nearest(*rels):
+        for rel in rels:
+            for f in both:
+                for r in both:
+                    b_pass_on(f, r, rel, True)
+
+    def b_rest(*rels):
+        for rel in rels:
+            for f in both:
+                for r in both:
+                    b_pass_on(f, r, rel, False)
+
+    def forward(r, j):
+        for f in both:
+            outer_forward(f, r, j)
+
+    def work(r, rel, **ends):
+        for f in both:
+            b_need(f, r, rel)
+            chunk(f, r, rel, **ends)
+
     for f in both:
         send(slot(f, 0, 0, 0), z_send.at[f], z_recv.at[f], device(x, y, up(z, 4, LINE), core))
         inner_start(f, 0)
@@ -222,21 +246,16 @@
         inner_finish(f, 0)
         b_start(f, 0)
         b_local(f, 0, 0)
-    for f in both:
-        outer_forward(f, 0, 0)
-    for f in both:
-        outer_forward(f, 0, 1)
+    forward(0, 0)
+    forward(0, 1)
     for f in both:
         arrived(slot(f, 1, 0, 0), z_recv.at[f])
         inner_start(f, 1)
         outer_send(f, 1, 0)
-    for f in both:
-        outer_forward(f, 0, 2)
-    for f in both:
-        for r in range(2):
-            b_relay(f, r, 0)
-    for f in both:
-        outer_forward(f, 0, 3)
+    forward(0, 2)
+    b_nearest(0)
+    forward(0, 3)
+    for f in both:
         for rel in (1, 2):
             b_start(f, rel)
             b_local(f, 0, rel)
@@ -246,41 +265,32 @@
         outer_finish(f, 0)
         b_start(f, 3)
         b_local(f, 0, 3)
+    b_rest(0)
     for f in both:
         inner_finish(f, 1)
         b_local(f, 1, 0)
-
-    def own_wait(f, r, rel):
-        pl.when(diagonal)(functools.partial(b_wait, f, r, rel))
-
-    for f in both:
-        outer_forward(f, 1, 0)
-        own_wait(f, 0, 0)
-        chunk(f, 0, 0, first=True)
-    for rel in (1, 2):
-        for f in both:
-            for r in range(2):
-                b_relay(f, r, rel)
-            outer_forward(f, 1, rel)
-            own_wait(f, 0, rel)
-            chunk(f, 0, rel)
-    for f in both:
-        for r in range(2):
-            b_relay(f, r, 3)
-        outer_forward(f, 1, 3)
+    forward(1, 0)
+    work(0, 0, first=True)
+    b_nearest(1, 2)
+    work(1, 0)
+    forward(1, 1)
+    b_rest(1, 2)
+    b_nearest(3)
+    forward(1, 2)
+    work(0, 1)
+    b_rest(3)
+    work(0, 2)
+    forward(1, 3)
     for f in both:
         for rel in (1, 2):
             b_local(f, 1, rel)
-        own_wait(f, 0, 3)
-        chunk(f, 0, 3)
-    for rel in (0, 1, 2):
-        for f in both:
-            own_wait(f, 1, rel)
-            chunk(f, 1, rel)
+    work(0, 3)
+    work(1, 1)
+    work(1, 2)
     for f in both:
         outer_finish(f, 1)
         b_local(f, 1, 3)
-        own_wait(f, 1, 3)
+        b_need(f, 1, 3)
         chunk(f, 1, 3, last=True)
 
     for copy, when in pending:
@@ -311,8 +321,9 @@
             dma((2, 2, 4)),
             dma((2, 2, 4, 4)),
             dma((2, 2, 4, 4)),
-            dma((2, 2, 4)),
-            dma((2, 2, 4)),
+            dma((2, 2, 2, 4)),
+            dma((2, 2, 4)),
+            dma((2, 2, 2, 4)),
             dma((2, 2, 4)),
             dma((2, 2, 4)),
         ],

time: 178 us -> 75.3 us (0.42)
  the two profiles are of different devices: /device:TPU:32 before, /device:TPU:48 now
where the time goes in v2:
time: 75.3 us; the launch traced here: 74.3 us
  Pallas kernels  70.4 us (93%)
  local copies, waits for them, and re-layouts  3.87 us (5%)
    pallas_call x1, Pallas kernels, on_device(): pl.pallas_call(functools.partial(kernel, norm), out_shape=jax.ShapeDtypeS...  70.4 us
    unnamed x5, local copies, waits for them, and re-layouts  3.87 us

profile of v2, /device:TPU:48, one launch (start us, length us, event | category | flops | bytes accessed | tf_op | source)
XLA Modules:
  0.0 74.3 jit_solution(18315859767372930205)
XLA Ops:
  0.0 0.0 copy-start
  0.0 0.9 %copy-done = bf16[4,32,1024]{2,1,0:T(8,128)(2,1)S(1)} copy-done((bf16[4,32,1024]{2,1,0:T(8,128)(2,1)S(1)}, bf16[4,32,1024]{2,1,0:T(8,128)(2,1)}, u32[]{:S(2)}) %copy-start) | copy-done | bytes 262168
  1.0 0.0 copy-start.1
  1.0 0.9 %copy-done.1 = s32[32,1024]{1,0:T(8,128)S(1)} copy-done((s32[32,1024]{1,0:T(8,128)S(1)}, s32[32,1024]{1,0:T(8,128)}, u32[]{:S(2)}) %copy-start.1) | copy-done | bytes 131096
  1.9 70.4 %shard_map.28 = f32[2,2,1024,256]{3,2,1,0:T(8,128)S(1)} custom-call(bf16[4,32,1024]{2,1,0:T(8,128)(2,1)S(1)} %copy-done, s32[32,1024]{1,0:T(8,128)S(1)} %copy-done.1), custom_call_target="tpu_custom_call" | custom-call | flops 4294967296 | bytes 4194304 | tf_op jit(solution)/shard_map/pallas_call | solution.py:310
  72.3 2.0 %copy.4 = f32[2,2,1024,256]{3,2,1,0:T(8,128)} copy(f32[2,2,1024,256]{3,2,1,0:T(8,128)S(1)} %shard_map.28) | data formatting | bytes 8388608
Async XLA Ops:
  0.0 0.9 %copy-start = (bf16[4,32,1024]{2,1,0:T(8,128)(2,1)S(1)}, bf16[4,32,1024]{2,1,0:T(8,128)(2,1)}, u32[]{:S(2)}) copy-start(bf16[4,32,1024]{2,1,0:T(8,128)(2,1)} %spectra.1) | copy-start | bytes 786436
  1.0 0.9 %copy-start.1 = (s32[32,1024]{1,0:T(8,128)S(1)}, s32[32,1024]{1,0:T(8,128)}, u32[]{:S(2)}) copy-start(s32[32,1024]{1,0:T(8,128)} %valid.1) | copy-start | bytes 393220

commit v3 on v2

--- a/solution.py
+++ b/solution.py
@@ -95,40 +95,56 @@
         inner, outer = place[f]
         return gathered.at[f, side(r), up(outer, do, RING), up(inner, di, RING)]
 
+    def plane_order(k):
+        return (k, 1 - k)
+
+    def outer_plane(f, r, j, k, p):
+        send(slot(f, r, 0, inner_steps[j]).at[p], out_send.at[r, f, k, j, p], out_recv.at[r, f, k, j, p],
+             ring_device(f, False, (1, -1)[k]))
+
     def outer_send(f, r, j):
-        block = slot(f, r, 0, inner_steps[j])
-        for k, step in enumerate((1, -1)):
-            send(block, out_send.at[r, f, k, j], out_recv.at[r, f, k, j], ring_device(f, False, step))
+        for n in range(2):
+            for k in range(2):
+                outer_plane(f, r, j, k, plane_order(k)[n])
 
     def inner_start(f, r):
         block = slot(f, r, 0, 0)
-        for k, step in enumerate((1, -1)):
-            send(block, in_send.at[r, f, k], in_recv.at[r, f, k], ring_device(f, True, step))
+        for n in range(2):
+            for k, step in enumerate((1, -1)):
+                p = plane_order(k)[n]
+                send(block.at[p], in_send.at[r, f, k, p], in_recv.at[r, f, k, p], ring_device(f, True, step))
 
     def inner_forward(f, r):
         for k, step in enumerate((1, -1)):
-            block = slot(f, r, 0, -step)
-            arrived(block, in_recv.at[r, f, k])
-            send(block.at[k], in_send.at[r, f, 2 + k], in_recv.at[r, f, 2 + k], ring_device(f, True, step))
+            plane = slot(f, r, 0, -step).at[k]
+            arrived(plane, in_recv.at[r, f, k, k])
+            send(plane, in_send.at[r, f, 2 + k, 0], in_recv.at[r, f, 2 + k, 0], ring_device(f, True, step))
+
+    def inner_rest(f, r):
+        for k, step in enumerate((1, -1)):
+            arrived(slot(f, r, 0, -step).at[1 - k], in_recv.at[r, f, k, 1 - k])
             outer_send(f, r, 1 + k)
 
     def inner_finish(f, r):
         block = slot(f, r, 0, 2)
         for k in range(2):
-            arrived(block.at[k], in_recv.at[r, f, 2 + k])
+            arrived(block.at[k], in_recv.at[r, f, 2 + k, 0])
         outer_send(f, r, 3)
 
     def outer_forward(f, r, j):
         for k, step in enumerate((1, -1)):
-            block = slot(f, r, -step, inner_steps[j])
-            arrived(block, out_recv.at[r, f, k, j])
-            send(block.at[k], out_send.at[r, f, 2 + k, j], out_recv.at[r, f, 2 + k, j], ring_device(f, False, step))
-
-    def outer_finish(f, r):
-        for j in range(4):
-            block = slot(f, r, 2, inner_steps[j])
-            for k in range(2):
-                arrived(block.at[k], out_recv.at[r, f, 2 + k, j])
+            plane = slot(f, r, -step, inner_steps[j]).at[k]
+            arrived(plane, out_recv.at[r, f, k, j, k])
+            send(plane, out_send.at[r, f, 2 + k, j, 0], out_recv.at[r, f, 2 + k, j, 0], ring_device(f, False, step))
+
+    def outer_rest(f, r, j):
+        for k, step in enumerate((1, -1)):
+            arrived(slot(f, r, -step, inner_steps[j]).at[1 - k], out_recv.at[r, f, k, j, 1 - k])
+
+    def outer_finish(f, r, j):
+        block = slot(f, r, 2, inner_steps[j])
+        for k in range(2):
+            arrived(block.at[k], out_recv.at[r, f, 2 + k, j, 0])
 
     diagonal = low == y
     owner = jnp.logical_and(diagonal, core == half)
@@ -140,10 +156,12 @@
     def b_slot(f, h, rel):
         return partner.at[f, h, up(place[f][1], outer_steps[rel], RING)]
 
-    def b_source(f, r, rel):
-        return gathered.at[f, side(r), up(place[f][1], outer_steps[rel], RING), :, :, :, lanes]
-
-    def b_start(f, rel):
+    def b_start(f, rel, j):
+        inner, outer = place[f]
+        outer = up(outer, outer_steps[rel], RING)
+        inner = up(inner, inner_steps[j], RING)
+        piece = gathered.at[f, half, outer, inner, :, :, lanes]
+        landing = partner.at[f, half, outer, inner]
         for k, step in enumerate((1, -1)):
             fits = [half_of(d * step) == core for d in (1, 2, 3)]
             nearest = jnp.where(fits[0], 1, jnp.where(fits[1], 2, 3))
@@ -151,14 +169,20 @@
             third = jnp.logical_and(fits[0], fits[2])
             for n, (distance, when) in enumerate(((nearest, found), (3, third))):
                 target = device(x, y, lax.rem(z + distance * step + LINE, LINE), f)
-                send(b_source(f, 0, rel), b_send.at[k, n, f, rel], b_recv.at[half, f, rel], target,
-                     landing=b_slot(f, half, rel), when=jnp.logical_and(diagonal, when))
-
-    def b_local(f, r, rel):
-        copy = pltpu.make_async_copy(b_source(f, r, rel), b_slot(f, side(r), rel), b_recv.at[side(r), f, rel])
-        pl.when(owner)(copy.start)
-        send(b_source(f, r, rel), b_side.at[r, f, rel], b_recv.at[side(r), f, rel], sibling,
-             landing=b_slot(f, side(r), rel), when=owner)
+                send(piece, b_send.at[k, n, f, rel, j], b_recv.at[half, f, rel], target,
+                     landing=landing, when=jnp.logical_and(diagonal, when))
+
+    def b_local(f, r, rel, j):
+        inner, outer = place[f]
+        outer = up(outer, outer_steps[rel], RING)
+        inner = up(inner, inner_steps[j], RING)
+
+        @pl.when(owner)
+        def _():
+            partner[f, side(r), outer, inner] = gathered[f, side(r), outer, inner, :, :, lanes]
+
+        send(gathered.at[f, side(r), outer, inner, :, :, lanes], b_side.at[r, f, rel, j],
+             b_recv.at[side(r), f, rel], sibling, landing=partner.at[f, side(r), outer, inner], when=owner)
 
     def b_wait(f, r, rel):
         arrived(b_slot(f, side(r), rel), b_recv.at[side(r), f, rel])
@@ -186,7 +210,8 @@
         send(block, b_far.at[int(nearest), r, f, rel], b_recv.at[h, f, rel], sibling, when=mine)
 
     def b_need(f, r, rel):
-        pl.when(jnp.logical_or(diagonal, core != f))(functools.partial(b_wait, f, r, rel))
+        needed = jnp.logical_or(jnp.logical_and(diagonal, core != half), jnp.logical_and(jnp.logical_not(diagonal), core != f))
+        pl.when(needed)(functools.partial(b_wait, f, r, rel))
 
     def chunk(f, r, rel, first=False, last=False):
         h = side(r)
@@ -195,22 +220,17 @@
         block = partner[f, h, outer]
         turned = jnp.stack([-block[:, 1], block[:, 0]], axis=1)
         right = jnp.concatenate([block.reshape(depth, width), turned.reshape(depth, width)], axis=1)
-        tile = 256
-
-        @pl.loop(0, gathered.shape[-1] // tile)
-        def _(t):
-            rows = pl.ds(pl.multiple_of(t * tile, tile), tile)
-            left = gathered[f, h, outer, :, :, :, rows].reshape(depth, tile)
-            product = lax.dot_general(
-                left, right, (((0,), (0,)), ((), ())), preferred_element_type=jnp.float32
-            )
-            for p in range(2):
-                part = product[:, p * width:(p + 1) * width]
-                if not first:
-                    part = out[p, f, rows, :] + part
-                if last:
-                    part = part * norm
-                out[p, f, rows, :] = part
+        left = gathered[f, h, outer].reshape(depth, gathered.shape[-1])
+        product = lax.dot_general(
+            left, right, (((0,), (0,)), ((), ())), preferred_element_type=jnp.float32
+        )
+        for p in range(2):
+            part = product[:, p * width:(p + 1) * width]
+            if not first:
+                part = out[p, f] + part
+            if last:
+                part = part * norm
+            out[p, f] = part
 
     both = range(2)
 
@@ -226,10 +246,6 @@
                 for r in both:
                     b_pass_on(f, r, rel, False)
 
-    def forward(r, j):
-        for f in both:
-            outer_forward(f, r, j)
-
     def work(r, rel, **ends):
         for f in both:
             b_need(f, r, rel)
@@ -237,61 +253,133 @@
 
     for f in both:
         send(slot(f, 0, 0, 0), z_send.at[f], z_recv.at[f], device(x, y, up(z, 4, LINE), core))
+    for f in both:
         inner_start(f, 0)
     for f in both:
         outer_send(f, 0, 0)
     for f in both:
         inner_forward(f, 0)
     for f in both:
+        inner_rest(f, 0)
+    for f in both:
         inner_finish(f, 0)
-        b_start(f, 0)
-        b_local(f, 0, 0)
-    forward(0, 0)
-    forward(0, 1)
+        b_start(f, 0, 0)
+        b_local(f, 0, 0, 0)
+        b_start(f, 0, 1)
+        b_local(f, 0, 0, 1)
+        b_start(f, 0, 2)
+        b_local(f, 0, 0, 2)
+        b_start(f, 0, 3)
+        b_local(f, 0, 0, 3)
+    for f in both:
+        outer_forward(f, 0, 0)
+    for f in both:
+        outer_rest(f, 0, 0)
+        b_start(f, 1, 0)
+        b_local(f, 0, 1, 0)
+        b_start(f, 2, 0)
+        b_local(f, 0, 2, 0)
+    for f in both:
+        outer_forward(f, 0, 1)
+    for f in both:
+        outer_rest(f, 0, 1)
+        b_start(f, 1, 1)
+        b_local(f, 0, 1, 1)
+        b_start(f, 2, 1)
+        b_local(f, 0, 2, 1)
     for f in both:
         arrived(slot(f, 1, 0, 0), z_recv.at[f])
         inner_start(f, 1)
         outer_send(f, 1, 0)
-    forward(0, 2)
+    for f in both:
+        outer_forward(f, 0, 2)
+    for f in both:
+        outer_rest(f, 0, 2)
+        b_start(f, 1, 2)
+        b_local(f, 0, 1, 2)
+        b_start(f, 2, 2)
+        b_local(f, 0, 2, 2)
     b_nearest(0)
-    forward(0, 3)
-    for f in both:
-        for rel in (1, 2):
-            b_start(f, rel)
-            b_local(f, 0, rel)
+    for f in both:
+        outer_forward(f, 0, 3)
+    for f in both:
+        outer_rest(f, 0, 3)
+        b_start(f, 1, 3)
+        b_local(f, 0, 1, 3)
+        b_start(f, 2, 3)
+        b_local(f, 0, 2, 3)
     for f in both:
         inner_forward(f, 1)
     for f in both:
-        outer_finish(f, 0)
-        b_start(f, 3)
-        b_local(f, 0, 3)
+        inner_rest(f, 1)
+    for f in both:
+        outer_finish(f, 0, 0)
+        b_start(f, 3, 0)
+        b_local(f, 0, 3, 0)
+        outer_finish(f, 0, 1)
+        b_start(f, 3, 1)
+        b_local(f, 0, 3, 1)
+        outer_finish(f, 0, 2)
+        b_start(f, 3, 2)
+        b_local(f, 0, 3, 2)
+        outer_finish(f, 0, 3)
+        b_start(f, 3, 3)
+        b_local(f, 0, 3, 3)
     b_rest(0)
     for f in both:
         inner_finish(f, 1)
-        b_local(f, 1, 0)
-    forward(1, 0)
+    for f in both:
+        b_local(f, 1, 0, 0)
+        b_local(f, 1, 0, 1)
+        b_local(f, 1, 0, 2)
+        b_local(f, 1, 0, 3)
+    for f in both:
+        outer_forward(f, 1, 0)
+    for f in both:
+        outer_forward(f, 1, 1)
+    for f in both:
+        outer_rest(f, 1, 0)
+        b_local(f, 1, 1, 0)
+        b_local(f, 1, 2, 0)
+    b_nearest(1)
+    b_nearest(2)
     work(0, 0, first=True)
-    b_nearest(1, 2)
     work(1, 0)
-    forward(1, 1)
-    b_rest(1, 2)
+    for f in both:
+        outer_forward(f, 1, 2)
+    for f in both:
+        outer_rest(f, 1, 1)
+        b_local(f, 1, 1, 1)
+        b_local(f, 1, 2, 1)
+    b_rest(1)
+    b_rest(2)
     b_nearest(3)
-    forward(1, 2)
+    for f in both:
+        outer_forward(f, 1, 3)
+    for f in both:
+        outer_rest(f, 1, 2)
+        b_local(f, 1, 1, 2)
+        b_local(f, 1, 2, 2)
+    for f in both:
+        outer_rest(f, 1, 3)
+        b_local(f, 1, 1, 3)
+        b_local(f, 1, 2, 3)
     work(0, 1)
     b_rest(3)
     work(0, 2)
-    forward(1, 3)
-    for f in both:
-        for rel in (1, 2):
-            b_local(f, 1, rel)
     work(0, 3)
     work(1, 1)
     work(1, 2)
     for f in both:
-        outer_finish(f, 1)
-        b_local(f, 1, 3)
-        b_need(f, 1, 3)
-        chunk(f, 1, 3, last=True)
+        outer_finish(f, 1, 0)
+        b_local(f, 1, 3, 0)
+        outer_finish(f, 1, 1)
+        b_local(f, 1, 3, 1)
+        outer_finish(f, 1, 2)
+        b_local(f, 1, 3, 2)
+        outer_finish(f, 1, 3)
+        b_local(f, 1, 3, 3)
+    work(1, 3, last=True)
 
     for copy, when in pending:
         if when is None:
@@ -317,14 +405,14 @@
             pltpu.VMEM((2, 2, RING, RING, 2, windows, width), jnp.bfloat16),
             dma((2,)),
             dma((2,)),
-            dma((2, 2, 4)),
-            dma((2, 2, 4)),
-            dma((2, 2, 4, 4)),
-            dma((2, 2, 4, 4)),
-            dma((2, 2, 2, 4)),
+            dma((2, 2, 4, 2)),
+            dma((2, 2, 4, 2)),
+            dma((2, 2, 4, 4, 2)),
+            dma((2, 2, 4, 4, 2)),
+            dma((2, 2, 2, 4, 4)),
             dma((2, 2, 4)),
             dma((2, 2, 2, 4)),
-            dma((2, 2, 4)),
+            dma((2, 2, 4, 4)),
             dma((2, 2, 4)),
         ],
         compiler_params=pltpu.CompilerParams(

time: 75.3 us -> 66.7 us (0.89); the launches traced: 74.3 us -> 66.6 us
  Pallas kernels: 70.4 us -> 62.7 us
    pallas_call x1, Pallas kernels: 70.4 us -> 62.7 us  [on_device(): pl.pallas_call(functools.partial(kernel, norm), out_shape=jax.ShapeDtypeS...]
where the time goes in v3:
time: 66.7 us; the launch traced here: 66.6 us
  Pallas kernels  62.7 us (94%)
  local copies, waits for them, and re-layouts  3.87 us (6%)
    pallas_call x1, Pallas kernels, on_device(): pl.pallas_call(functools.partial(kernel, norm), out_shape=jax.ShapeDtypeS...  62.7 us
    unnamed x5, local copies, waits for them, and re-layouts  3.87 us

profile of v3, /device:TPU:48, one launch (start us, length us, event | category | flops | bytes accessed | tf_op | source)
XLA Modules:
  0.0 66.6 jit_solution(916611822670501932)
XLA Ops:
  0.0 0.0 copy-start
  0.0 0.9 %copy-done = bf16[4,32,1024]{2,1,0:T(8,128)(2,1)S(1)} copy-done((bf16[4,32,1024]{2,1,0:T(8,128)(2,1)S(1)}, bf16[4,32,1024]{2,1,0:T(8,128)(2,1)}, u32[]{:S(2)}) %copy-start) | copy-done | bytes 262168
  1.0 0.0 copy-start.1
  1.0 0.9 %copy-done.1 = s32[32,1024]{1,0:T(8,128)S(1)} copy-done((s32[32,1024]{1,0:T(8,128)S(1)}, s32[32,1024]{1,0:T(8,128)}, u32[]{:S(2)}) %copy-start.1) | copy-done | bytes 131096
  1.9 62.7 %shard_map.28 = f32[2,2,1024,256]{3,2,1,0:T(8,128)S(1)} custom-call(bf16[4,32,1024]{2,1,0:T(8,128)(2,1)S(1)} %copy-done, s32[32,1024]{1,0:T(8,128)S(1)} %copy-done.1), custom_call_target="tpu_custom_call" | custom-call | flops 4294967296 | bytes 4194304 | tf_op jit(solution)/shard_map/pallas_call | solution.py:398
  64.6 2.0 %copy.4 = f32[2,2,1024,256]{3,2,1,0:T(8,128)} copy(f32[2,2,1024,256]{3,2,1,0:T(8,128)S(1)} %shard_map.28) | data formatting | bytes 8388608
Async XLA Ops:
  0.0 0.9 %copy-start = (bf16[4,32,1024]{2,1,0:T(8,128)(2,1)S(1)}, bf16[4,32,1024]{2,1,0:T(8,128)(2,1)}, u32[]{:S(2)}) copy-start(bf16[4,32,1024]{2,1,0:T(8,128)(2,1)} %spectra.1) | copy-start | bytes 786436
  1.0 0.9 %copy-start.1 = (s32[32,1024]{1,0:T(8,128)S(1)}, s32[32,1024]{1,0:T(8,128)}, u32[]{:S(2)}) copy-start(s32[32,1024]{1,0:T(8,128)} %valid.1) | copy-start | bytes 393220

commit v4 on v3

--- a/solution.py
+++ b/solution.py
@@ -20,8 +20,8 @@
     return lax.rem(a + (d + n), n)
 
 
-def kernel(norm, spectra, valid, out, gathered, partner, z_send, z_recv, in_send, in_recv,
-           out_send, out_recv, b_send, b_pass, b_far, b_side, b_recv):
+def kernel(norm, spectra, valid, out, gathered, partner, a_send, z_recv, in_recv, out_recv,
+           b_send, b_pass, b_far, b_side, b_recv):
     row = lax.axis_index("row")
     col = lax.axis_index("col")
     core = lax.rem(row, 2)
@@ -58,8 +58,6 @@
         gathered[f, half, outer, inner, 0] = (real * factor).astype(jnp.bfloat16)
         gathered[f, half, outer, inner, 1] = (imag * factor).astype(jnp.bfloat16)
     pl.semaphore_wait(barrier, len(greeted))
-
-    pending = []
 
     def send(ref, send_sem, recv_sem, target, landing=None, when=None):
         copy = pltpu.make_async_remote_copy(
@@ -74,13 +72,12 @@
             copy.start()
         else:
             pl.when(when)(copy.start)
-        pending.append((copy, when))
 
     def arrived(ref, recv_sem):
         pltpu.make_async_remote_copy(
             src_ref=ref,
             dst_ref=ref,
-            send_sem=z_send.at[0],
+            send_sem=a_send.at[4],
             recv_sem=recv_sem,
             device_id=sibling,
             device_id_type=MESH,
@@ -99,7 +96,7 @@
         return (k, 1 - k)
 
     def outer_plane(f, r, j, k, p):
-        send(slot(f, r, 0, inner_steps[j]).at[p], out_send.at[r, f, k, j, p], out_recv.at[r, f, k, j, p],
+        send(slot(f, r, 0, inner_steps[j]).at[p], a_send.at[2], out_recv.at[r, f, k, j, p],
              ring_device(f, False, (1, -1)[k]))
 
     def outer_send(f, r, j):
@@ -112,13 +109,13 @@
         for n in range(2):
             for k, step in enumerate((1, -1)):
                 p = plane_order(k)[n]
-                send(block.at[p], in_send.at[r, f, k, p], in_recv.at[r, f, k, p], ring_device(f, True, step))
+                send(block.at[p], a_send.at[0], in_recv.at[r, f, k, p], ring_device(f, True, step))
 
     def inner_forward(f, r):
         for k, step in enumerate((1, -1)):
             plane = slot(f, r, 0, -step).at[k]
             arrived(plane, in_recv.at[r, f, k, k])
-            send(plane, in_send.at[r, f, 2 + k, 0], in_recv.at[r, f, 2 + k, 0], ring_device(f, True, step))
+            send(plane, a_send.at[1], in_recv.at[r, f, k, 2], ring_device(f, True, step))
 
     def inner_rest(f, r):
         for k, step in enumerate((1, -1)):
@@ -128,14 +125,14 @@
     def inner_finish(f, r):
         block = slot(f, r, 0, 2)
         for k in range(2):
-            arrived(block.at[k], in_recv.at[r, f, 2 + k, 0])
+            arrived(block.at[k], in_recv.at[r, f, k, 2])
         outer_send(f, r, 3)
 
     def outer_forward(f, r, j):
         for k, step in enumerate((1, -1)):
             plane = slot(f, r, -step, inner_steps[j]).at[k]
             arrived(plane, out_recv.at[r, f, k, j, k])
-            send(plane, out_send.at[r, f, 2 + k, j, 0], out_recv.at[r, f, 2 + k, j, 0], ring_device(f, False, step))
+            send(plane, a_send.at[3], out_recv.at[r, f, k, j, 2], ring_device(f, False, step))
 
     def outer_rest(f, r, j):
         for k, step in enumerate((1, -1)):
@@ -144,7 +141,7 @@
     def outer_finish(f, r, j):
         block = slot(f, r, 2, inner_steps[j])
         for k in range(2):
-            arrived(block.at[k], out_recv.at[r, f, 2 + k, j, 0])
+            arrived(block.at[k], out_recv.at[r, f, k, j, 2])
 
     diagonal = low == y
     owner = jnp.logical_and(diagonal, core == half)
@@ -155,6 +152,15 @@
 
     def b_slot(f, h, rel):
         return partner.at[f, h, up(place[f][1], outer_steps[rel], RING)]
+
+    def b_targets():
+        for k, step in enumerate((1, -1)):
+            fits = [half_of(d * step) == core for d in (1, 2, 3)]
+            nearest = jnp.where(fits[0], 1, jnp.where(fits[1], 2, 3))
+            found = jnp.logical_or(fits[0], jnp.logical_or(fits[1], fits[2]))
+            third = jnp.logical_and(fits[0], fits[2])
+            yield k, 0, nearest * step, jnp.logical_and(diagonal, found)
+            yield k, 1, 3 * step, jnp.logical_and(diagonal, third)
 
     def b_start(f, rel, j):
         inner, outer = place[f]
@@ -162,15 +168,9 @@
         inner = up(inner, inner_steps[j], RING)
         piece = gathered.at[f, half, outer, inner, :, :, lanes]
         landing = partner.at[f, half, outer, inner]
-        for k, step in enumerate((1, -1)):
-            fits = [half_of(d * step) == core for d in (1, 2, 3)]
-            nearest = jnp.where(fits[0], 1, jnp.where(fits[1], 2, 3))
-            found = jnp.logical_or(fits[0], jnp.logical_or(fits[1], fits[2]))
-            third = jnp.logical_and(fits[0], fits[2])
-            for n, (distance, when) in enumerate(((nearest, found), (3, third))):
-                target = device(x, y, lax.rem(z + distance * step + LINE, LINE), f)
-                send(piece, b_send.at[k, n, f, rel, j], b_recv.at[half, f, rel], target,
-                     landing=landing, when=jnp.logical_and(diagonal, when))
+        for k, n, distance, when in b_targets():
+            target = device(x, y, lax.rem(z + distance + LINE, LINE), f)
+            send(piece, b_send.at[k, n], b_recv.at[half, f, rel], target, landing=landing, when=when)
 
     def b_local(f, r, rel, j):
         inner, outer = place[f]
@@ -181,7 +181,7 @@
         def _():
             partner[f, side(r), outer, inner] = gathered[f, side(r), outer, inner, :, :, lanes]
 
-        send(gathered.at[f, side(r), outer, inner, :, :, lanes], b_side.at[r, f, rel, j],
+        send(gathered.at[f, side(r), outer, inner, :, :, lanes], b_side.at[0],
              b_recv.at[side(r), f, rel], sibling, landing=partner.at[f, side(r), outer, inner], when=owner)
 
     def b_wait(f, r, rel):
@@ -197,17 +197,20 @@
         goes_on = jnp.logical_and(nearest, jnp.logical_and(steps != 3, lax.div(after, 4) == half))
         return nearest, goes_on, after
 
+    def b_mine(f, r, nearest):
+        is_nearest, goes_on, after = b_place(r)
+        mine = jnp.logical_and(jnp.logical_not(diagonal), core == f)
+        mine = jnp.logical_and(mine, is_nearest if nearest else jnp.logical_not(is_nearest))
+        return mine, jnp.logical_and(mine, goes_on), after
+
     def b_pass_on(f, r, rel, nearest):
         h = side(r)
         block = b_slot(f, h, rel)
-        is_nearest, goes_on, after = b_place(r)
-        mine = jnp.logical_and(jnp.logical_not(diagonal), core == f)
-        mine = jnp.logical_and(mine, is_nearest if nearest else jnp.logical_not(is_nearest))
+        mine, goes_on, after = b_mine(f, r, nearest)
         pl.when(mine)(functools.partial(b_wait, f, r, rel))
         if nearest:
-            send(block, b_pass.at[r, f, rel], b_recv.at[h, f, rel], device(x, y, after, core),
-                 when=jnp.logical_and(mine, goes_on))
-        send(block, b_far.at[int(nearest), r, f, rel], b_recv.at[h, f, rel], sibling, when=mine)
+            send(block, b_pass.at[r, f], b_recv.at[h, f, rel], device(x, y, after, core), when=goes_on)
+        send(block, b_far.at[int(nearest), r, f], b_recv.at[h, f, rel], sibling, when=mine)
 
     def b_need(f, r, rel):
         needed = jnp.logical_or(jnp.logical_and(diagonal, core != half), jnp.logical_and(jnp.logical_not(diagonal), core != f))
@@ -252,7 +255,7 @@
             chunk(f, r, rel, **ends)
 
     for f in both:
-        send(slot(f, 0, 0, 0), z_send.at[f], z_recv.at[f], device(x, y, up(z, 4, LINE), core))
+        send(slot(f, 0, 0, 0), a_send.at[4], z_recv.at[f], device(x, y, up(z, 4, LINE), core))
     for f in both:
         inner_start(f, 0)
     for f in both:
@@ -381,11 +384,35 @@
         b_local(f, 1, 3, 3)
     work(1, 3, last=True)
 
-    for copy, when in pending:
+    def drain(ref, send_sem, when=None):
+        wait = pltpu.make_async_remote_copy(
+            src_ref=ref,
+            dst_ref=ref,
+            send_sem=send_sem,
+            recv_sem=z_recv.at[0],
+            device_id=sibling,
+            device_id_type=MESH,
+        ).wait_send
         if when is None:
-            copy.wait_send()
+            wait()
         else:
-            pl.when(when)(copy.wait_send)
+            pl.when(when)(wait)
+
+    drain(gathered.at[0, 0, pl.ds(0, 2)], a_send.at[0])
+    drain(gathered.at[0, 0, 0], a_send.at[1])
+    drain(gathered.at[0], a_send.at[2])
+    drain(gathered.at[0, 0], a_send.at[3])
+    drain(gathered.at[0, 0, 0, pl.ds(0, 2)], a_send.at[4])
+    drain(partner, b_side.at[0], owner)
+    for k, n, _, when in b_targets():
+        drain(partner.at[0], b_send.at[k, n], when)
+    for r in both:
+        for f in both:
+            for nearest in (True, False):
+                mine, goes_on, _ = b_mine(f, r, nearest)
+                drain(partner.at[0, 0], b_far.at[int(nearest), r, f], mine)
+                if nearest:
+                    drain(partner.at[0, 0], b_pass.at[r, f], goes_on)
 
 
 def on_device(spectra, valid):
@@ -403,16 +430,14 @@
         scratch_shapes=[
             pltpu.VMEM((2, 2, RING, RING, 2, windows, rows), jnp.bfloat16),
             pltpu.VMEM((2, 2, RING, RING, 2, windows, width), jnp.bfloat16),
+            dma((5,)),
             dma((2,)),
-            dma((2,)),
-            dma((2, 2, 4, 2)),
-            dma((2, 2, 4, 2)),
-            dma((2, 2, 4, 4, 2)),
-            dma((2, 2, 4, 4, 2)),
-            dma((2, 2, 2, 4, 4)),
-            dma((2, 2, 4)),
-            dma((2, 2, 2, 4)),
-            dma((2, 2, 4, 4)),
+            dma((2, 2, 2, 3)),
+            dma((2, 2, 2, 4, 3)),
+            dma((2, 2)),
+            dma((2, 2)),
+            dma((2, 2, 2)),
+            dma((1,)),
             dma((2, 2, 4)),
         ],
         compiler_params=pltpu.CompilerParams(

time: 66.7 us -> 62.6 us (0.939)
  Pallas kernels: 62.7 us -> 58.6 us
    pallas_call x1, Pallas kernels: 62.7 us -> 58.6 us  [on_device(): pl.pallas_call(functools.partial(kernel, norm), out_shape=jax.ShapeDtypeS...]
where the time goes in v4:
time: 62.6 us; the launch traced here: 62.5 us
  Pallas kernels  58.6 us (94%)
  local copies, waits for them, and re-layouts  3.87 us (6%)
    pallas_call x1, Pallas kernels, on_device(): pl.pallas_call(functools.partial(kernel, norm), out_shape=jax.ShapeDtypeS...  58.6 us
    unnamed x5, local copies, waits for them, and re-layouts  3.87 us

profile of v4, /device:TPU:48, one launch (start us, length us, event | category | flops | bytes accessed | tf_op | source)
XLA Modules:
  0.0 62.5 jit_solution(6008525575109732116)
XLA Ops:
  0.0 0.0 copy-start
  0.0 0.9 %copy-done = bf16[4,32,1024]{2,1,0:T(8,128)(2,1)S(1)} copy-done((bf16[4,32,1024]{2,1,0:T(8,128)(2,1)S(1)}, bf16[4,32,1024]{2,1,0:T(8,128)(2,1)}, u32[]{:S(2)}) %copy-start) | copy-done | bytes 262168
  1.0 0.0 copy-start.1
  1.0 0.9 %copy-done.1 = s32[32,1024]{1,0:T(8,128)S(1)} copy-done((s32[32,1024]{1,0:T(8,128)S(1)}, s32[32,1024]{1,0:T(8,128)}, u32[]{:S(2)}) %copy-start.1) | copy-done | bytes 131096
  1.9 58.6 %shard_map.28 = f32[2,2,1024,256]{3,2,1,0:T(8,128)S(1)} custom-call(bf16[4,32,1024]{2,1,0:T(8,128)(2,1)S(1)} %copy-done, s32[32,1024]{1,0:T(8,128)S(1)} %copy-done.1), custom_call_target="tpu_custom_call" | custom-call | flops 4294967296 | bytes 4194304 | tf_op jit(solution)/shard_map/pallas_call | solution.py:425
  60.5 2.0 %copy.4 = f32[2,2,1024,256]{3,2,1,0:T(8,128)} copy(f32[2,2,1024,256]{3,2,1,0:T(8,128)S(1)} %shard_map.28) | data formatting | bytes 8388608
Async XLA Ops:
  0.0 0.9 %copy-start = (bf16[4,32,1024]{2,1,0:T(8,128)(2,1)S(1)}, bf16[4,32,1024]{2,1,0:T(8,128)(2,1)}, u32[]{:S(2)}) copy-start(bf16[4,32,1024]{2,1,0:T(8,128)(2,1)} %spectra.1) | copy-start | bytes 786436
  1.0 0.9 %copy-start.1 = (s32[32,1024]{1,0:T(8,128)S(1)}, s32[32,1024]{1,0:T(8,128)}, u32[]{:S(2)}) copy-start(s32[32,1024]{1,0:T(8,128)} %valid.1) | copy-start | bytes 393220

commit v5 on v4

--- a/solution.py
+++ b/solution.py
@@ -20,8 +20,8 @@
     return lax.rem(a + (d + n), n)
 
 
-def kernel(norm, spectra, valid, out, gathered, partner, a_send, z_recv, in_recv, out_recv,
-           b_send, b_pass, b_far, b_side, b_recv):
+def kernel(norm, spectra, valid, out, gathered, partner, a_send, z_recv, in_recv, far_recv,
+           out_recv, rest_recv, last_recv, b_send, b_pass, b_far, b_side, b_recv):
     row = lax.axis_index("row")
     col = lax.axis_index("col")
     core = lax.rem(row, 2)
@@ -43,11 +43,56 @@
     sibling = device(x, y, z, 1 - core)
 
     barrier = pltpu.get_barrier_semaphore()
-    greeted = [ring_device(0, inner, step) for inner in (True, False) for step in (1, -1)]
-    greeted += [device(x, y, up(z, d, LINE), c) for d in range(1, LINE) for c in range(2)]
-    greeted.append(sibling)
-    for other in greeted:
-        pl.semaphore_signal(barrier, inc=1, device_id=other, device_id_type=MESH)
+    diagonal = low == y
+    owner = jnp.logical_and(diagonal, core == half)
+
+    def greet(other, when=None):
+        signal = functools.partial(
+            pl.semaphore_signal, barrier, inc=1, device_id=other, device_id_type=MESH
+        )
+        if when is None:
+            signal()
+        else:
+            pl.when(when)(signal)
+
+    def half_of(d):
+        return lax.div(up(z, d, LINE), 4)
+
+    def b_place(h):
+        distance = lax.rem(z - (y + 4 * h) + 2 * LINE, LINE)
+        step = jnp.where(distance < 4, 1, -1)
+        steps = jnp.where(distance < 4, distance, LINE - distance)
+        before = lax.rem(z - step + LINE, LINE)
+        second = lax.rem(z - 2 * step + LINE, LINE)
+        after = lax.rem(z + step + LINE, LINE)
+        nearest = jnp.logical_or(steps == 1, lax.div(before, 4) != half)
+        goes_on = jnp.logical_and(nearest, jnp.logical_and(steps != 3, lax.div(after, 4) == half))
+        straight = jnp.logical_or(nearest, jnp.logical_and(steps == 3, lax.div(second, 4) == half))
+        return nearest, goes_on, straight, before, after
+
+    def b_targets():
+        for k, step in enumerate((1, -1)):
+            fits = [half_of(d * step) == core for d in (1, 2, 3)]
+            nearest = jnp.where(fits[0], 1, jnp.where(fits[1], 2, 3))
+            found = jnp.logical_or(fits[0], jnp.logical_or(fits[1], fits[2]))
+            third = jnp.logical_and(fits[0], fits[2])
+            yield k, 0, nearest * step, jnp.logical_and(diagonal, found)
+            yield k, 1, 3 * step, jnp.logical_and(diagonal, third)
+
+    off_diagonal = jnp.logical_not(diagonal)
+    for inner in (True, False):
+        for step in (1, -1):
+            greet(ring_device(0, inner, step))
+    greet(device(x, y, up(z, 4, LINE), core))
+    greet(sibling, jnp.logical_not(owner))
+    copies_to = 5 + jnp.where(jnp.logical_or(off_diagonal, owner), 1, 0)
+    for h in range(2):
+        _, goes_on, straight, before, _ = b_place(h)
+        sender = device(x, y, jnp.where(straight, y + 4 * h, before), jnp.where(straight, half, core))
+        greet(sender, off_diagonal)
+        copies_to += jnp.where(jnp.logical_and(off_diagonal, goes_on), 1, 0)
+    for _, _, _, found in b_targets():
+        copies_to += jnp.where(found, 2, 0)
 
     for f in range(2):
         real = spectra[2 * f].astype(jnp.float32)
@@ -57,7 +102,7 @@
         inner, outer = place[f]
         gathered[f, half, outer, inner, 0] = (real * factor).astype(jnp.bfloat16)
         gathered[f, half, outer, inner, 1] = (imag * factor).astype(jnp.bfloat16)
-    pl.semaphore_wait(barrier, len(greeted))
+    pl.semaphore_wait(barrier, copies_to)
 
     def send(ref, send_sem, recv_sem, target, landing=None, when=None):
         copy = pltpu.make_async_remote_copy(
@@ -96,7 +141,8 @@
         return (k, 1 - k)
 
     def outer_plane(f, r, j, k, p):
-        send(slot(f, r, 0, inner_steps[j]).at[p], a_send.at[2], out_recv.at[r, f, k, j, p],
+        recv_sem = out_recv.at[r, f, k, j] if p == k else rest_recv.at[r, f, j]
+        send(slot(f, r, 0, inner_steps[j]).at[p], a_send.at[2], recv_sem,
              ring_device(f, False, (1, -1)[k]))
 
     def outer_send(f, r, j):
@@ -115,7 +161,7 @@
         for k, step in enumerate((1, -1)):
             plane = slot(f, r, 0, -step).at[k]
             arrived(plane, in_recv.at[r, f, k, k])
-            send(plane, a_send.at[1], in_recv.at[r, f, k, 2], ring_device(f, True, step))
+            send(plane, a_send.at[1], far_recv.at[r, f], ring_device(f, True, step))
 
     def inner_rest(f, r):
         for k, step in enumerate((1, -1)):
@@ -124,43 +170,25 @@
 
     def inner_finish(f, r):
         block = slot(f, r, 0, 2)
-        for k in range(2):
-            arrived(block.at[k], in_recv.at[r, f, k, 2])
+        arrived(block, far_recv.at[r, f])
         outer_send(f, r, 3)
 
     def outer_forward(f, r, j):
         for k, step in enumerate((1, -1)):
             plane = slot(f, r, -step, inner_steps[j]).at[k]
-            arrived(plane, out_recv.at[r, f, k, j, k])
-            send(plane, a_send.at[3], out_recv.at[r, f, k, j, 2], ring_device(f, False, step))
+            arrived(plane, out_recv.at[r, f, k, j])
+            send(plane, a_send.at[3], last_recv.at[r, f, j], ring_device(f, False, step))
 
     def outer_rest(f, r, j):
-        for k, step in enumerate((1, -1)):
-            arrived(slot(f, r, -step, inner_steps[j]).at[1 - k], out_recv.at[r, f, k, j, 1 - k])
+        arrived(slot(f, r, -1, inner_steps[j]), rest_recv.at[r, f, j])
 
     def outer_finish(f, r, j):
-        block = slot(f, r, 2, inner_steps[j])
-        for k in range(2):
-            arrived(block.at[k], out_recv.at[r, f, k, j, 2])
-
-    diagonal = low == y
-    owner = jnp.logical_and(diagonal, core == half)
+        arrived(slot(f, r, 2, inner_steps[j]), last_recv.at[r, f, j])
+
     outer_steps = (0, -1, 1, 2)
-
-    def half_of(d):
-        return lax.div(up(z, d, LINE), 4)
 
     def b_slot(f, h, rel):
         return partner.at[f, h, up(place[f][1], outer_steps[rel], RING)]
-
-    def b_targets():
-        for k, step in enumerate((1, -1)):
-            fits = [half_of(d * step) == core for d in (1, 2, 3)]
-            nearest = jnp.where(fits[0], 1, jnp.where(fits[1], 2, 3))
-            found = jnp.logical_or(fits[0], jnp.logical_or(fits[1], fits[2]))
-            third = jnp.logical_and(fits[0], fits[2])
-            yield k, 0, nearest * step, jnp.logical_and(diagonal, found)
-            yield k, 1, 3 * step, jnp.logical_and(diagonal, third)
 
     def b_start(f, rel, j):
         inner, outer = place[f]
@@ -187,19 +215,9 @@
     def b_wait(f, r, rel):
         arrived(b_slot(f, side(r), rel), b_recv.at[side(r), f, rel])
 
-    def b_place(r):
-        distance = lax.rem(z - (y + 4 * side(r)) + 2 * LINE, LINE)
-        step = jnp.where(distance < 4, 1, -1)
-        steps = jnp.where(distance < 4, distance, LINE - distance)
-        before = lax.rem(z - step + LINE, LINE)
-        after = lax.rem(z + step + LINE, LINE)
-        nearest = jnp.logical_or(steps == 1, lax.div(before, 4) != half)
-        goes_on = jnp.logical_and(nearest, jnp.logical_and(steps != 3, lax.div(after, 4) == half))
-        return nearest, goes_on, after
-
     def b_mine(f, r, nearest):
-        is_nearest, goes_on, after = b_place(r)
-        mine = jnp.logical_and(jnp.logical_not(diagonal), core == f)
+        is_nearest, goes_on, _, _, after = b_place(side(r))
+        mine = jnp.logical_and(off_diagonal, core == f)
         mine = jnp.logical_and(mine, is_nearest if nearest else jnp.logical_not(is_nearest))
         return mine, jnp.logical_and(mine, goes_on), after
 
@@ -432,8 +450,11 @@
             pltpu.VMEM((2, 2, RING, RING, 2, windows, width), jnp.bfloat16),
             dma((5,)),
             dma((2,)),
-            dma((2, 2, 2, 3)),
-            dma((2, 2, 2, 4, 3)),
+            dma((2, 2, 2, 2)),
+            dma((2, 2)),
+            dma((2, 2, 2, 4)),
+            dma((2, 2, 4)),
+            dma((2, 2, 4)),
             dma((2, 2)),
             dma((2, 2)),
             dma((2, 2, 2)),

time: 62.6 us -> 61.6 us (0.984)
  Pallas kernels: 58.6 us -> 57.6 us
    pallas_call x1, Pallas kernels: 58.6 us -> 57.6 us  [on_device(): pl.pallas_call(functools.partial(kernel, norm), out_shape=jax.ShapeDtypeS...]
where the time goes in v5:
time: 61.6 us; the launch traced here: 61.5 us
  Pallas kernels  57.6 us (94%)
  local copies, waits for them, and re-layouts  3.87 us (6%)
    pallas_call x1, Pallas kernels, on_device(): pl.pallas_call(functools.partial(kernel, norm), out_shape=jax.ShapeDtypeS...  57.6 us
    unnamed x5, local copies, waits for them, and re-layouts  3.87 us

profile of v5, /device:TPU:48, one launch (start us, length us, event | category | flops | bytes accessed | tf_op | source)
XLA Modules:
  0.0 61.5 jit_solution(12728054998232630586)
XLA Ops:
  0.0 0.0 copy-start
  0.0 0.9 %copy-done = bf16[4,32,1024]{2,1,0:T(8,128)(2,1)S(1)} copy-done((bf16[4,32,1024]{2,1,0:T(8,128)(2,1)S(1)}, bf16[4,32,1024]{2,1,0:T(8,128)(2,1)}, u32[]{:S(2)}) %copy-start) | copy-done | bytes 262168
  1.0 0.0 copy-start.1
  1.0 0.9 %copy-done.1 = s32[32,1024]{1,0:T(8,128)S(1)} copy-done((s32[32,1024]{1,0:T(8,128)S(1)}, s32[32,1024]{1,0:T(8,128)}, u32[]{:S(2)}) %copy-start.1) | copy-done | bytes 131096
  1.9 57.6 %shard_map.28 = f32[2,2,1024,256]{3,2,1,0:T(8,128)S(1)} custom-call(bf16[4,32,1024]{2,1,0:T(8,128)(2,1)S(1)} %copy-done, s32[32,1024]{1,0:T(8,128)S(1)} %copy-done.1), custom_call_target="tpu_custom_call" | custom-call | flops 4294967296 | bytes 4194304 | tf_op jit(solution)/shard_map/pallas_call | solution.py:443
  59.5 2.0 %copy.4 = f32[2,2,1024,256]{3,2,1,0:T(8,128)} copy(f32[2,2,1024,256]{3,2,1,0:T(8,128)S(1)} %shard_map.28) | data formatting | bytes 8388608
Async XLA Ops:
  0.0 0.9 %copy-start = (bf16[4,32,1024]{2,1,0:T(8,128)(2,1)S(1)}, bf16[4,32,1024]{2,1,0:T(8,128)(2,1)}, u32[]{:S(2)}) copy-start(bf16[4,32,1024]{2,1,0:T(8,128)(2,1)} %spectra.1) | copy-start | bytes 786436
  1.0 0.9 %copy-start.1 = (s32[32,1024]{1,0:T(8,128)S(1)}, s32[32,1024]{1,0:T(8,128)}, u32[]{:S(2)}) copy-start(s32[32,1024]{1,0:T(8,128)} %valid.1) | copy-start | bytes 393220

commit v6 on v5

--- a/solution.py
+++ b/solution.py
@@ -20,7 +20,7 @@
     return lax.rem(a + (d + n), n)
 
 
-def kernel(norm, spectra, valid, out, gathered, partner, a_send, z_recv, in_recv, far_recv,
+def kernel(norm, white_a, white_b, white_c, white_d, out, gathered, partner, a_send, z_recv, in_recv, far_recv,
            out_recv, rest_recv, last_recv, b_send, b_pass, b_far, b_side, b_recv):
     row = lax.axis_index("row")
     col = lax.axis_index("col")
@@ -31,7 +31,7 @@
     y = lax.div(col, 8)
     z = half * 4 + low
     width = partner.shape[-1]
-    windows = spectra.shape[1]
+    windows = white_a.shape[0]
     lanes = pl.ds(pl.multiple_of(x * width, width), width)
     place = ((x, y), (y, x))
 
@@ -94,14 +94,10 @@
     for _, _, _, found in b_targets():
         copies_to += jnp.where(found, 2, 0)
 
-    for f in range(2):
-        real = spectra[2 * f].astype(jnp.float32)
-        imag = spectra[2 * f + 1].astype(jnp.float32)
-        amplitude = jnp.sqrt(real * real + imag * imag)
-        factor = valid[...].astype(jnp.float32) / jnp.maximum(amplitude, 0.5)
+    for f, planes in enumerate(((white_a, white_b), (white_c, white_d))):
         inner, outer = place[f]
-        gathered[f, half, outer, inner, 0] = (real * factor).astype(jnp.bfloat16)
-        gathered[f, half, outer, inner, 1] = (imag * factor).astype(jnp.bfloat16)
+        for p in range(2):
+            gathered[f, half, outer, inner, p] = planes[p][...]
     pl.semaphore_wait(barrier, copies_to)
 
     def send(ref, send_sem, recv_sem, target, landing=None, when=None):
@@ -320,7 +316,6 @@
         b_local(f, 0, 1, 2)
         b_start(f, 2, 2)
         b_local(f, 0, 2, 2)
-    b_nearest(0)
     for f in both:
         outer_forward(f, 0, 3)
     for f in both:
@@ -329,6 +324,7 @@
         b_local(f, 0, 1, 3)
         b_start(f, 2, 3)
         b_local(f, 0, 2, 3)
+    b_nearest(0)
     for f in both:
         inner_forward(f, 1)
     for f in both:
@@ -346,7 +342,6 @@
         outer_finish(f, 0, 3)
         b_start(f, 3, 3)
         b_local(f, 0, 3, 3)
-    b_rest(0)
     for f in both:
         inner_finish(f, 1)
     for f in both:
@@ -358,16 +353,17 @@
         outer_forward(f, 1, 0)
     for f in both:
         outer_forward(f, 1, 1)
+    b_rest(0)
     for f in both:
         outer_rest(f, 1, 0)
         b_local(f, 1, 1, 0)
         b_local(f, 1, 2, 0)
     b_nearest(1)
     b_nearest(2)
+    for f in both:
+        outer_forward(f, 1, 2)
     work(0, 0, first=True)
     work(1, 0)
-    for f in both:
-        outer_forward(f, 1, 2)
     for f in both:
         outer_rest(f, 1, 1)
         b_local(f, 1, 1, 1)
@@ -375,8 +371,10 @@
     b_rest(1)
     b_rest(2)
     b_nearest(3)
+    work(0, 1)
     for f in both:
         outer_forward(f, 1, 3)
+    work(0, 2)
     for f in both:
         outer_rest(f, 1, 2)
         b_local(f, 1, 1, 2)
@@ -385,9 +383,7 @@
         outer_rest(f, 1, 3)
         b_local(f, 1, 1, 3)
         b_local(f, 1, 2, 3)
-    work(0, 1)
     b_rest(3)
-    work(0, 2)
     work(0, 3)
     work(1, 1)
     work(1, 2)
@@ -433,6 +429,17 @@
                     drain(partner.at[0, 0], b_pass.at[r, f], goes_on)
 
 
+def whiten(spectra, valid):
+    kept = valid.astype(jnp.float32)
+    white = []
+    for f in range(2):
+        real = spectra[2 * f].astype(jnp.float32)
+        imag = spectra[2 * f + 1].astype(jnp.float32)
+        factor = kept / jnp.maximum(jnp.sqrt(real * real + imag * imag), 0.5)
+        white += [(real * factor).astype(jnp.bfloat16), (imag * factor).astype(jnp.bfloat16)]
+    return white
+
+
 def on_device(spectra, valid):
     planes, windows, rows = spectra.shape
     width = rows // 4
@@ -443,7 +450,7 @@
     return pl.pallas_call(
         functools.partial(kernel, norm),
         out_shape=jax.ShapeDtypeStruct((2, planes // 2, rows, width), jnp.float32),
-        in_specs=[vmem, vmem],
+        in_specs=[vmem] * 4,
         out_specs=vmem,
         scratch_shapes=[
             pltpu.VMEM((2, 2, RING, RING, 2, windows, rows), jnp.bfloat16),
@@ -467,7 +474,7 @@
         cost_estimate=pl.CostEstimate(
             flops=16 * total * rows * width, bytes_accessed=2**22, transcendentals=0
         ),
-    )(spectra, valid)
+    )(*whiten(spectra, valid))
 
 
 def solution(mesh):

time: 61.6 us -> 60.6 us (0.984)
  local copies, waits for them, and re-layouts: 3.87 us -> 2.02 us
  other arithmetic: 0 us -> 1.2 us
  Pallas kernels: 57.6 us -> 56.9 us
    unnamed x5 -> x1, local copies, waits for them, and re-layouts: 3.87 us -> 2.02 us
    convert_element_type x0 -> x1, other arithmetic: none -> 1.2 us  [whiten(): (imag * factor).astype(jnp.bfloat16)]
    pallas_call x1, Pallas kernels: 57.6 us -> 56.9 us  [on_device(): pl.pallas_call(functools.partial(kernel, norm), out_shape=jax.ShapeDtypeS...]
where the time goes in v6:
time: 60.6 us; the launch traced here: 60.2 us
  Pallas kernels  56.9 us (94%)
  local copies, waits for them, and re-layouts  2.02 us (3%)
  other arithmetic  1.2 us (2%)
    pallas_call x1, Pallas kernels, on_device(): pl.pallas_call(functools.partial(kernel, norm), out_shape=jax.ShapeDtypeS...  56.9 us
    unnamed x1, local copies, waits for them, and re-layouts  2.02 us

profile of v6, /device:TPU:48, one launch (start us, length us, event | category | flops | bytes accessed | tf_op | source)
XLA Modules:
  0.0 60.2 jit_solution(523831842789620031)
XLA Ops:
  0.0 1.2 %fusion.11 = (bf16[32,1024]{1,0:T(8,128)(2,1)S(1)}, bf16[32,1024]{1,0:T(8,128)(2,1)S(1)}, bf16[32,1024]{1,0:T(8,128)(2,1)S(1)}, bf16[32,1024]{1,0:T(8,128)(2,1)S(1)}) fusion(bf16[4,32,1024]{2,1,0:T(8,128)(2,1)} %param.2, s32[32,1024]{1,0:T(8,128)} %param.3), kind=kLoop, calls=%fused_computation.19 | loop fusion | flops 753664 | bytes 655360 | tf_op jit(solution)/shard_map/convert_element_type | solution.py:439
  1.2 56.9 %shard_map.28 = f32[2,2,1024,256]{3,2,1,0:T(8,128)S(1)} custom-call(bf16[32,1024]{1,0:T(8,128)(2,1)S(1)} %get-tuple-element.6.white_a, bf16[32,1024]{1,0:T(8,128)(2,1)S(1)} %get-tuple-element.7.white_b, bf16[32,1024]{1,0:T(8,128)(2,1)S(1)} %get-tuple-element.8.white_c, bf16[32,1024]{1,0:T(8,128)(2,1)S(1)} %get-tuple-element.5.white_d), custom_call_target="tpu_custom_call" | custom-call | flops 4294967296 | bytes 4194304 | tf_op jit(solution)/shard_map/pallas_call | solution.py:450
  58.2 2.0 %copy.4 = f32[2,2,1024,256]{3,2,1,0:T(8,128)} copy(f32[2,2,1024,256]{3,2,1,0:T(8,128)S(1)} %shard_map.28) | data formatting | bytes 8388608

commit v7 on v6

--- a/solution.py
+++ b/solution.py
@@ -333,12 +333,15 @@
         outer_finish(f, 0, 0)
         b_start(f, 3, 0)
         b_local(f, 0, 3, 0)
+    for f in both:
         outer_finish(f, 0, 1)
         b_start(f, 3, 1)
         b_local(f, 0, 3, 1)
+    for f in both:
         outer_finish(f, 0, 2)
         b_start(f, 3, 2)
         b_local(f, 0, 3, 2)
+    for f in both:
         outer_finish(f, 0, 3)
         b_start(f, 3, 3)
         b_local(f, 0, 3, 3)
@@ -390,10 +393,13 @@
     for f in both:
         outer_finish(f, 1, 0)
         b_local(f, 1, 3, 0)
+    for f in both:
         outer_finish(f, 1, 1)
         b_local(f, 1, 3, 1)
+    for f in both:
         outer_finish(f, 1, 2)
         b_local(f, 1, 3, 2)
+    for f in both:
         outer_finish(f, 1, 3)
         b_local(f, 1, 3, 3)
     work(1, 3, last=True)

time: 60.6 us -> 60.6 us (level)
  no operation moved by 1% of the time
where the time goes in v7:
time: 60.6 us; the launch traced here: 60.2 us
  Pallas kernels  56.9 us (94%)
  local copies, waits for them, and re-layouts  2.02 us (3%)
  other arithmetic  1.2 us (2%)
    pallas_call x1, Pallas kernels, on_device(): pl.pallas_call(functools.partial(kernel, norm), out_shape=jax.ShapeDtypeS...  56.9 us
    unnamed x1, local copies, waits for them, and re-layouts  2.02 us

profile of v7, /device:TPU:48, one launch (start us, length us, event | category | flops | bytes accessed | tf_op | source)
XLA Modules:
  0.0 60.2 jit_solution(12526705288415489002)
XLA Ops:
  0.0 1.2 %fusion.11 = (bf16[32,1024]{1,0:T(8,128)(2,1)S(1)}, bf16[32,1024]{1,0:T(8,128)(2,1)S(1)}, bf16[32,1024]{1,0:T(8,128)(2,1)S(1)}, bf16[32,1024]{1,0:T(8,128)(2,1)S(1)}) fusion(bf16[4,32,1024]{2,1,0:T(8,128)(2,1)} %param.2, s32[32,1024]{1,0:T(8,128)} %param.3), kind=kLoop, calls=%fused_computation.19 | loop fusion | flops 753664 | bytes 655360 | tf_op jit(solution)/shard_map/convert_element_type | solution.py:445
  1.2 56.9 %shard_map.28 = f32[2,2,1024,256]{3,2,1,0:T(8,128)S(1)} custom-call(bf16[32,1024]{1,0:T(8,128)(2,1)S(1)} %get-tuple-element.6.white_a, bf16[32,1024]{1,0:T(8,128)(2,1)S(1)} %get-tuple-element.7.white_b, bf16[32,1024]{1,0:T(8,128)(2,1)S(1)} %get-tuple-element.8.white_c, bf16[32,1024]{1,0:T(8,128)(2,1)S(1)} %get-tuple-element.5.white_d), custom_call_target="tpu_custom_call" | custom-call | flops 4294967296 | bytes 4194304 | tf_op jit(solution)/shard_map/pallas_call | solution.py:456
  58.2 2.0 %copy.4 = f32[2,2,1024,256]{3,2,1,0:T(8,128)} copy(f32[2,2,1024,256]{3,2,1,0:T(8,128)S(1)} %shard_map.28) | data formatting | bytes 8388608
